TPU v7x, 128 devices: a whole 4x4x4 slice. The times are simulated.
128 devices in a mesh: gz: 32 (over z, y, core), gx: 4 (over x).
Axes of the slice: x: 4, y: 4, z: 4, core: 2. Of those that a mesh axis runs over, the one named last changes fastest.
Arguments:
- fields: bfloat16 [64, 128, 32, 64], P(None, 'gz', 'gx'), may hold values from -6 to 6
- block_patch: int32 [32, 32], P('gz', 'gx'), may hold values from -1 to 127, as said below
- fine_in: bfloat16 [32, 32, 64, 512], P('gz', 'gx'), may hold values from -6 to 6
- conv_first: bfloat16 [27, 64, 64], replicated, may hold values from -0.15625 to 0.15625
- restrict_weight: bfloat16 [8, 64, 64], replicated, may hold values from -0.25 to 0.25
- coarse_weight: bfloat16 [27, 64, 64], replicated, may hold values from -0.15625 to 0.15625
- prolong_weight: bfloat16 [8, 64, 64], replicated, may hold values from -0.75 to 0.75
- conv_second: bfloat16 [27, 64, 64], replicated, may hold values from -0.15625 to 0.15625
- refine_weight: bfloat16 [27, 64, 64], replicated, may hold values from -0.15625 to 0.15625
Outputs:
- base_out: bfloat16 [64, 128, 32, 64], P(None, 'gz', 'gx')
- fine_out: bfloat16 [32, 32, 64, 512], P('gz', 'gx')
Inputs may be any that keep to these rules, and one draw needn't show every extreme that they name: `block_patch`: entry [g, (k * 4 + h) * 2 + s] is -1 for an empty slot or the index py * 16 + px of a patch of slab g whose row py lies in h * 2 to (h + 1) * 2 - 1. The patches named in one slab are distinct. Within each group of 2 slots the live ones come first, and group (g, k, k) has one or more live slots.
All inputs are finite; a program needn't handle non-finite values.
Results may differ from a plain program's by a relative error of at most 0.007.
Values may be sent and summed in bfloat16 or wider, within the bound.
A program may use at most 128 MiB of HBM per device.

v0:
```python
import functools

import jax
import jax.numpy as jnp
import numpy as np
from jax import lax
from jax.experimental import pallas as pl
from jax.experimental.pallas import tpu as pltpu
from jax.sharding import PartitionSpec as P

BF = jnp.bfloat16
F32 = jnp.float32
MESH = pl.DeviceIdType.MESH
DIRS = [(dz, dy) for dz in (-1, 0, 1) for dy in (-1, 0, 1) if (dz, dy) != (0, 0)]


def split_table():
    cell = np.arange(512)
    row, col = cell // 64, cell % 64
    table = np.zeros((512, 512), np.float32)
    table[cell, ((row % 2) * 2 + col % 2) * 128 + (row // 2) * 32 + col // 2] = 1
    return table


def spread_table():
    table = np.zeros((128, 512), np.float32)
    for q in range(2):
        for r in range(2):
            for k in range(32):
                table[k, (q * 2 + r) * 128 + q * 64 + 2 * k + r] = 1
    return table


def mean_table():
    cell = np.arange(512)
    z, y, x = cell // 64, cell // 8 % 8, cell % 8
    table = np.zeros((512, 128), np.float32)
    table[cell, (z // 2) * 16 + (y // 2) * 4 + x // 2] = 0.125
    return table


def block_table():
    table = np.zeros((5, 256, 1152), np.float32)
    for m in range(5):
        for tap in range(9):
            for a in range(2):
                for b in range(8):
                    for e in range(8):
                        y, x = b + tap // 3 - 1, e + tap % 3 - 1
                        col = tap * 128 + a * 64 + b * 8 + e
                        ghost = (y // 2 + 1) * 6 + x // 2 + 1
                        if m == 4:
                            table[m, a * 128 + (0, 80)[a] + ghost, col] = 1
                        elif 0 <= y < 8 and 0 <= x < 8:
                            table[m, a * 64 + y * 8 + x, col] = 1
                        else:
                            table[m, 128 + 40 * ((m + 1) % 3) + ghost, col] = 1
    return table


def dot(a, b):
    return jnp.dot(a, b, preferred_element_type=F32)


def silu(v):
    return v / (1.0 + jnp.exp(-v))


def lanes_of(shape):
    return lax.broadcasted_iota(jnp.int32, shape, len(shape) - 1)


def splat(flag, shape):
    return jnp.full(shape, jnp.where(flag, 1.0, 0.0).astype(F32), F32)


def pack_taps(raw, packed):
    for dz in range(3):
        packed[dz * 64 : dz * 64 + 64, :] = jnp.concatenate(
            [raw[dz * 9 + t] for t in range(9)], axis=1
        )


def shifted(tile, period):
    lane = lanes_of(tile.shape) % period
    zero = jnp.zeros_like(tile)
    left = jnp.where(lane != 0, pltpu.roll(tile, 1, 1), zero)
    right = jnp.where(lane != period - 1, pltpu.roll(tile, 127, 1), zero)
    return left, tile, right


def stack_rows(tiles, first, last, x_ref):
    low = lanes_of((64, 128)) < 64
    moved = [shifted(t, 64) for t in tiles]
    for dx in range(3):
        swapped = [pltpu.roll(m[dx], 64, 1) for m in moved]
        count = len(tiles)
        between = [
            jnp.where(low, swapped[max(j, 0)], swapped[min(j + 1, count - 1)])
            for j in range(-1, count)
        ]
        for j in range(first, last):
            at = slice((j - first) * 128, (j - first) * 128 + 128)
            x_ref[dx * 64 : dx * 64 + 64, at] = between[j]
            x_ref[192 + dx * 64 : 256 + dx * 64, at] = moved[j][dx]
            x_ref[384 + dx * 64 : 448 + dx * 64, at] = between[j + 1]


def kernel(
    fields,
    patch,
    fine,
    w_first,
    w_restrict,
    w_coarse,
    w_prolong,
    w_second,
    w_refine,
    t_split,
    t_spread,
    t_mean,
    t_block,
    base_out,
    fine_out,
    fields_v,
    cells,
    field_t,
    raw_first,
    raw_restrict,
    raw_coarse,
    raw_prolong,
    raw_second,
    raw_refine,
    split_v,
    spread_v,
    mean_v,
    block_v,
    fine_v,
    fine_o,
    k_first,
    k_restrict,
    k_coarse,
    k_prolong,
    k_second,
    k_refine,
    lists,
    live_v,
    pick,
    place,
    x_v,
    y_v,
    act,
    summed,
    coarse_i,
    coarse_o,
    xc_v,
    u_v,
    win_o,
    win_i,
    xf_v,
    ret_o,
    ret_i,
    load_sem,
    store_sem,
    s_send,
    s_recv,
    c_send,
    c_recv,
    o_send,
    o_recv,
    l_send,
    l_recv,
    w_send,
    w_recv,
    r_send,
    r_recv,
):
    g = lax.axis_index("gz")
    h = lax.axis_index("gx")
    n_g = lax.axis_size("gz")
    n_h = lax.axis_size("gx")

    def near(dz, dy):
        return (lax.rem(g + dz + n_g, n_g), lax.rem(h + dy + n_h, n_h))

    barrier = pltpu.get_barrier_semaphore()
    partners = DIRS + [(0, 2)]
    for dz, dy in partners:
        pl.semaphore_signal(barrier, inc=1, device_id=near(dz, dy), device_id_type=MESH)

    loads = []
    for i, (src, dst) in enumerate(
        [
            (fields, fields_v),
            (w_first, raw_first),
            (w_restrict, raw_restrict),
            (w_coarse, raw_coarse),
            (t_split, split_v),
            (fine, fine_v),
            (w_refine, raw_refine),
            (t_block, block_v),
            (w_prolong, raw_prolong),
            (w_second, raw_second),
            (t_spread, spread_v),
            (t_mean, mean_v),
        ]
    ):
        loads.append(pltpu.make_async_copy(src, dst, load_sem.at[i]))
        loads[-1].start()

    lists[h] = jnp.zeros((8, 128), jnp.int32)
    lists[h, 0:1, 0:8] = patch[...]

    loads[0].wait()
    cells[...] = fields_v[...].astype(F32).reshape(2048, 64)
    for z in range(4):
        for j in range(4):
            pair = [cells[pl.ds(z * 8 + 2 * j + q, 64, stride=32), :] for q in range(2)]
            field_t[2 + z, 1 + j] = jnp.concatenate(pair, axis=1).astype(BF)

    pl.semaphore_wait(barrier, len(partners))

    def span_of(d, own, width, low, high):
        if d == 0:
            return pl.ds(low, own), pl.ds(low, own)
        if d > 0:
            return pl.ds(low + own - width, width), pl.ds(low - width, width)
        return pl.ds(low, width), pl.ds(high, width)

    sends = []
    for i, (dz, dy) in enumerate(DIRS):
        zs, zd = span_of(dz, 4, 2, 2, 6)
        ys, yd = span_of(dy, 4, 1, 1, 5)
        sends.append(
            pltpu.make_async_remote_copy(
                src_ref=field_t.at[zs, ys],
                dst_ref=field_t.at[zd, yd],
                send_sem=s_send.at[i],
                recv_sem=s_recv.at[i],
                device_id=near(dz, dy),
                device_id_type=MESH,
            )
        )
    for copy in sends:
        copy.start()
    list_sends = []
    for d in range(1, 4):
        list_sends.append(
            pltpu.make_async_remote_copy(
                src_ref=lists.at[h],
                dst_ref=lists.at[h],
                send_sem=l_send.at[d - 1],
                recv_sem=l_recv.at[d - 1],
                device_id=near(0, d),
                device_id_type=MESH,
            )
        )
        list_sends[-1].start()

    for copy in loads[1:]:
        copy.wait()
    pack_taps(raw_first, k_first)
    pack_taps(raw_coarse, k_coarse)
    pack_taps(raw_second, k_second)
    pack_taps(raw_refine, k_refine)
    k_restrict[...] = jnp.concatenate([raw_restrict[t] for t in range(8)], axis=1)
    for p in range(2):
        k_prolong[p * 64 : p * 64 + 64, :] = jnp.concatenate(
            [raw_prolong[p * 4 + t] for t in range(4)], axis=1
        )

    for copy in list_sends:
        copy.wait_recv()
    entry = lax.broadcasted_iota(jnp.int32, (8, 128), 1)
    own = patch[...].astype(F32)
    for s in range(8):
        mine = jnp.sum(
            jnp.where(lanes_of((1, 8)) == s, own, 0.0), axis=1, keepdims=True
        )
        live_v[s : s + 1, :] = jnp.where(jnp.broadcast_to(mine, (1, 128)) >= 0.0, 1.0, 0.0)
    lane = lanes_of((1, 128)).astype(F32)
    line = jnp.floor((lane + 0.5) * (1.0 / 6.0))
    place_x = lane - 6.0 * line - 1.0
    source = lax.broadcasted_iota(jnp.int32, (768, 128), 0).astype(F32)
    target = lanes_of((64, 512)).astype(F32)
    inner = (lax.broadcasted_iota(jnp.int32, (64, 1), 0) % 16).astype(F32)
    inner_y = jnp.floor(inner * 0.25)
    inner = inner_y * 64.0 + (inner - 4.0 * inner_y)
    for k in range(4):
        ids = lists[k].astype(F32)
        for s in range(2):
            at = k * 2 + s
            value = jnp.sum(
                jnp.where(entry == h * 2 + s, ids, 0.0), axis=1, keepdims=True
            )[0:1]
            py = jnp.floor(value * (1.0 / 16.0))
            px4 = 4.0 * (value - 16.0 * py)
            top = 256.0 * (py - 2.0 * h.astype(F32))
            col = place_x + px4
            want = jnp.where(
                (lane < 36.0) & (col >= 0.0) & (col < 64.0),
                (line + 1.0) * 64.0 + col + top,
                -1.0,
            )
            pick[:, at * 128 : at * 128 + 128] = jnp.where(source == want, 1.0, 0.0).astype(BF)
            want = jnp.where(value >= 0.0, inner + px4 + top, -1.0)
            place[at * 64 : at * 64 + 64, :] = jnp.where(target == want, 1.0, 0.0).astype(BF)

    for copy in sends:
        copy.wait_recv()

    first_z, last_z = g == 0, g == n_g - 1
    ok_low = splat(h != 0, (64, 128)).astype(BF)
    ok_high = splat(h != n_h - 1, (64, 128)).astype(BF)

    def conv_first_plane(p, carry):
        out = ((p < 2) & first_z) | ((p >= 6) & last_z)
        ok = splat(jnp.logical_not(out), (64, 128)).astype(BF)
        tiles = [field_t[p, t] * ok for t in range(6)]
        tiles[0] = tiles[0] * ok_low
        tiles[5] = tiles[5] * ok_high
        stack_rows(tiles, 0, 6, x_v)
        y_v[p] = dot(k_first[...], x_v[...])
        return carry

    lax.fori_loop(0, 8, conv_first_plane, 0)

    def first_active(q, carry):
        out = ((q == 0) & first_z) | ((q == 5) & last_z)
        for t in range(6):
            at = slice(t * 128, t * 128 + 128)
            total = y_v[q, 0:64, at] + y_v[q + 1, 64:128, at] + y_v[q + 2, 128:192, at]
            ok = jnp.logical_not(out)
            if t == 0:
                ok = ok & (h != 0)
            if t == 5:
                ok = ok & (h != n_h - 1)
            act[pl.ds(q * 64, 64), at] = (silu(total) * splat(ok, (64, 128))).astype(BF)
        return carry

    lax.fori_loop(0, 6, first_active, 0)

    parted = dot(act[64:320, 128:640], split_v[...]).astype(BF)
    gathered = jnp.concatenate(
        [
            jnp.concatenate(
                [
                    parted[(2 * i + p) * 64 : (2 * i + p) * 64 + 64, f * 128 : f * 128 + 128]
                    for p in range(2)
                    for f in range(4)
                ],
                axis=0,
            )
            for i in range(2)
        ],
        axis=1,
    )
    reduced = dot(k_restrict[...], gathered).astype(BF)
    coarse_i[1, 1] = reduced[:, 0:128]
    coarse_i[2, 1] = reduced[:, 128:256]

    def coarse_copies(buffer, send_sem, recv_sem):
        copies = []
        for i, (dz, dy) in enumerate(DIRS):
            zs, zd = span_of(dz, 2, 1, 1, 3)
            copies.append(
                pltpu.make_async_remote_copy(
                    src_ref=buffer.at[zs, pl.ds(1, 1)],
                    dst_ref=buffer.at[zd, pl.ds(1 - dy, 1)],
                    send_sem=send_sem.at[i],
                    recv_sem=recv_sem.at[i],
                    device_id=near(dz, dy),
                    device_id_type=MESH,
                )
            )
        return copies

    in_sends = coarse_copies(coarse_i, c_send, c_recv)
    for copy in in_sends:
        copy.start()

    def block_windows(k, carry):
        at = pl.ds(pl.multiple_of(k * 256, 128), 256)
        found = dot(act[...], pick[:, at])
        for s in range(2):
            parts = [found[q * 64 : q * 64 + 64, s * 128 : s * 128 + 128] for q in range(6)]
            for t in range(2):
                tile = (
                    parts[3 * t]
                    + pltpu.roll(parts[3 * t + 1], 40, 1)
                    + pltpu.roll(parts[3 * t + 2], 80, 1)
                )
                win_o[t, k, s] = tile.astype(BF)
        return carry

    lax.fori_loop(0, 4, block_windows, 0)
    win_sends = []
    for d in range(1, 4):
        peer = near(0, d)
        win_sends.append(
            pltpu.make_async_remote_copy(
                src_ref=win_o.at[:, peer[1]],
                dst_ref=win_i.at[:, h],
                send_sem=w_send.at[d - 1],
                recv_sem=w_recv.at[d - 1],
                device_id=peer,
                device_id_type=MESH,
            )
        )
        win_sends[-1].start()
    for t in range(2):
        for s in range(2):
            win_i[t, h, s] = win_o[t, h, s]

    for copy in in_sends:
        copy.wait_recv()

    def coarse_tiles(buffer, i):
        tiles = [buffer[i, t] for t in range(3)]
        if i in (0, 3):
            ok = splat(jnp.logical_not(first_z if i == 0 else last_z), (64, 128)).astype(BF)
            tiles = [t * ok for t in tiles]
        return [tiles[0] * ok_low, tiles[1], tiles[2] * ok_high]

    quarter = lanes_of((64, 128))
    for i in range(4):
        before, mid, after = coarse_tiles(coarse_i, i)
        up = jnp.where(quarter < 32, pltpu.roll(before, 32, 1), pltpu.roll(mid, 32, 1))
        down = jnp.where(quarter < 96, pltpu.roll(mid, 96, 1), pltpu.roll(after, 96, 1))
        for dy, tile in enumerate((up, mid, down)):
            for dx, moved in enumerate(shifted(tile, 32)):
                tap = dy * 3 + dx
                xc_v[tap * 64 : tap * 64 + 64, i * 128 : i * 128 + 128] = moved
    total = dot(k_coarse[...], xc_v[...])
    for i in range(2):
        value = (
            total[0:64, i * 128 : i * 128 + 128]
            + total[64:128, i * 128 + 128 : i * 128 + 256]
            + total[128:192, i * 128 + 256 : i * 128 + 384]
        )
        coarse_o[1 + i, 1] = silu(value).astype(BF)
    out_sends = coarse_copies(coarse_o, o_send, o_recv)
    for copy in out_sends:
        copy.start()

    for copy in win_sends:
        copy.wait_recv()
    for m in range(5):
        if m < 4:
            left = fine_v[0, :, :, m * 128 : m * 128 + 128].reshape(512, 128)
            right = win_i[(m + 1) // 3].reshape(512, 128)
        else:
            left = win_i[0].reshape(512, 128)
            right = win_i[1].reshape(512, 128)
        spread = dot(jnp.concatenate([left, right], axis=1), block_v[m]).astype(BF)
        for s in range(8):
            for tap in range(9):
                xf_v[s, tap * 64 : tap * 64 + 64, m * 128 : m * 128 + 128] = spread[
                    s * 64 : s * 64 + 64, tap * 128 : tap * 128 + 128
                ]
    low = lanes_of((64, 128)) < 64

    def refine(s, carry):
        total = dot(k_refine[...], xf_v[s])
        alive = live_v[pl.ds(s, 1), :] > 0.5
        behind = [total[0:64, m * 128 : m * 128 + 128] for m in range(5)]
        ahead = [total[128:192, m * 128 : m * 128 + 128] for m in range(5)]
        behind_r = [pltpu.roll(v, 64, 1) for v in behind[:4]]
        ahead_r = [pltpu.roll(v, 64, 1) for v in ahead[:4]]
        for m in range(4):
            at = slice(m * 128, m * 128 + 128)
            value = total[64:128, at]
            value += jnp.where(low, behind_r[m - 1] if m > 0 else behind[4], behind_r[m])
            value += jnp.where(low, ahead_r[m], ahead_r[m + 1] if m < 3 else ahead[4])
            value += fine_v[0, s, :, at].astype(F32)
            value = jnp.where(jnp.broadcast_to(alive, (64, 128)), value, 0.0)
            fine_o[0, s, :, at] = value.astype(BF)
        return carry

    lax.fori_loop(0, 8, refine, 0)
    fine_store = pltpu.make_async_copy(fine_o, fine_out, store_sem.at[0])
    fine_store.start()
    means = dot(fine_o[0].reshape(512, 512), mean_v[...])
    for k in range(4):
        ret_o[k] = (
            means[k * 128 : k * 128 + 64] + pltpu.roll(means[k * 128 + 64 : k * 128 + 128], 64, 1)
        ).astype(BF)
    ret_sends = []
    for d in range(1, 4):
        peer = near(0, d)
        ret_sends.append(
            pltpu.make_async_remote_copy(
                src_ref=ret_o.at[peer[1]],
                dst_ref=ret_i.at[h],
                send_sem=r_send.at[d - 1],
                recv_sem=r_recv.at[d - 1],
                device_id=peer,
                device_id_type=MESH,
            )
        )
        ret_sends[-1].start()
    ret_i[h] = ret_o[h]

    for copy in out_sends:
        copy.wait_recv()
    for i in range(4):
        before, mid, after = coarse_tiles(coarse_o, i)
        rows = [pltpu.roll(before, 32, 1), mid]
        rows += [pltpu.roll(mid, 128 - 32 * j, 1) for j in range(1, 4)]
        rows.append(after)
        spread = dot(jnp.concatenate(rows, axis=0), spread_v[...]).astype(BF)
        for j in range(6):
            for f in range(4):
                u_v[f * 64 : f * 64 + 64, j * 128 : j * 128 + 128] = spread[
                    j * 64 : j * 64 + 64, f * 128 : f * 128 + 128
                ]
        lifted = dot(k_prolong[...], u_v[...])
        for p in range(2):
            q = 2 * i - 1 + p
            if 0 <= q <= 5:
                at = slice(q * 64, q * 64 + 64)
                summed[at, :] = (
                    act[at, :].astype(F32) + lifted[p * 64 : p * 64 + 64, :]
                ).astype(BF)

    def conv_second_plane(q, carry):
        at = pl.ds(pl.multiple_of(q * 64, 64), 64)
        tiles = [summed[at, t * 128 : t * 128 + 128] for t in range(6)]
        stack_rows(tiles, 1, 5, x_v)
        y_v[q, :, 0:512] = dot(k_second[...], x_v[:, 0:512])
        return carry

    lax.fori_loop(0, 6, conv_second_plane, 0)

    for copy in ret_sends:
        copy.wait_recv()
    wide = lanes_of((64, 512)) % 64 // 16
    back = jnp.concatenate([ret_i[k] for k in range(4)], axis=1)
    zero = jnp.zeros_like(back)
    ones = jnp.where(lanes_of((16, 512)) % 64 < 16, 1.0, 0.0).astype(BF)
    stacked = jnp.concatenate([jnp.where(wide == z, back, zero) for z in range(4)] + [ones], axis=0)
    placed = dot(stacked, place[...])
    for z in range(4):
        for j in range(4):
            at = slice(j * 128, j * 128 + 128)
            value = y_v[z, 0:64, at] + y_v[z + 1, 64:128, at] + y_v[z + 2, 128:192, at]
            value += field_t[2 + z, 1 + j].astype(F32)
            covered = jnp.broadcast_to(placed[256:257, at], (64, 128)) > 0.5
            value = jnp.where(covered, placed[z * 64 : z * 64 + 64, at], value)
            cells[pl.ds(z * 8 + 2 * j, 64, stride=32), :] = value[:, 0:64]
            cells[pl.ds(z * 8 + 2 * j + 1, 64, stride=32), :] = value[:, 64:128]
    fields_v[...] = cells[...].reshape(64, 4, 8, 64).astype(BF)
    base_store = pltpu.make_async_copy(fields_v, base_out, store_sem.at[1])
    base_store.start()
    for copy in sends + list_sends + in_sends + win_sends + out_sends + ret_sends:
        copy.wait_send()
    fine_store.wait()
    base_store.wait()


def body(
    fields,
    block_patch,
    fine_in,
    conv_first,
    restrict_weight,
    coarse_weight,
    prolong_weight,
    conv_second,
    refine_weight,
):
    any_spec = pl.BlockSpec(memory_space=pl.ANY)
    vmem_spec = pl.BlockSpec(memory_space=pltpu.VMEM)
    dma = pltpu.SemaphoreType.DMA
    v = pltpu.VMEM
    return pl.pallas_call(
        kernel,
        out_shape=[
            jax.ShapeDtypeStruct(fields.shape, BF),
            jax.ShapeDtypeStruct(fine_in.shape, BF),
        ],
        in_specs=[any_spec, vmem_spec] + [any_spec] * 11,
        out_specs=[any_spec, any_spec],
        scratch_shapes=[
            v((64, 4, 8, 64), BF),
            v((2048, 64), F32),
            v((8, 6, 64, 128), BF),
            v((27, 64, 64), BF),
            v((8, 64, 64), BF),
            v((27, 64, 64), BF),
            v((8, 64, 64), BF),
            v((27, 64, 64), BF),
            v((27, 64, 64), BF),
            v((512, 512), BF),
            v((128, 512), BF),
            v((512, 128), BF),
            v((5, 256, 1152), BF),
            v((1, 8, 64, 512), BF),
            v((1, 8, 64, 512), BF),
            v((192, 576), BF),
            v((64, 512), BF),
            v((192, 576), BF),
            v((128, 256), BF),
            v((192, 576), BF),
            v((192, 576), BF),
            v((4, 8, 128), jnp.int32),
            v((8, 128), F32),
            v((768, 1024), BF),
            v((512, 512), BF),
            v((576, 768), BF),
            v((8, 192, 768), F32),
            v((384, 768), BF),
            v((384, 768), BF),
            v((4, 3, 64, 128), BF),
            v((4, 3, 64, 128), BF),
            v((576, 512), BF),
            v((256, 768), BF),
            v((2, 4, 2, 64, 128), BF),
            v((2, 4, 2, 64, 128), BF),
            v((8, 576, 640), BF),
            v((4, 64, 128), BF),
            v((4, 64, 128), BF),
            dma((12,)),
            dma((2,)),
            dma((8,)),
            dma((8,)),
            dma((8,)),
            dma((8,)),
            dma((8,)),
            dma((8,)),
            dma((3,)),
            dma((3,)),
            dma((3,)),
            dma((3,)),
            dma((3,)),
            dma((3,)),
        ],
        compiler_params=pltpu.CompilerParams(
            collective_id=0, has_side_effects=True, vmem_limit_bytes=52 * 1024 * 1024
        ),
        cost_estimate=pl.CostEstimate(flops=8 * 10**9, bytes_accessed=8 * 10**6, transcendentals=0),
    )(
        fields,
        block_patch,
        fine_in,
        conv_first,
        restrict_weight,
        coarse_weight,
        prolong_weight,
        conv_second,
        refine_weight,
        jnp.asarray(split_table(), BF),
        jnp.asarray(spread_table(), BF),
        jnp.asarray(mean_table(), BF),
        jnp.asarray(block_table(), BF),
    )


def solution(mesh):
    in_specs = (
        P(None, "gz", "gx", None),
        P("gz", "gx"),
        P("gz", "gx", None, None),
        P(),
        P(),
        P(),
        P(),
        P(),
        P(),
    )
    out_specs = (P(None, "gz", "gx", None), P("gz", "gx", None, None))
    return jax.shard_map(body, mesh=mesh, in_specs=in_specs, out_specs=out_specs, check_vma=False)
```

profile of v0, /device:TPU:0, one launch (start us, length us, event | category | flops | bytes accessed | tf_op | source)
XLA Modules:
  0.0 51.8 jit_solution(14009236251919123894)
XLA Ops:
  0.6 0.0 copy-start
  0.6 1.0 %copy-done = bf16[27,64,64]{2,1,0:T(8,128)(2,1)S(1)} copy-done((bf16[27,64,64]{2,1,0:T(8,128)(2,1)S(1)}, bf16[27,64,64]{2,1,0:T(8,128)(2,1)}, u32[]{:S(2)}) %copy-start) | copy-done | bytes 221208
  1.6 0.0 copy-start.1
  1.6 1.0 %copy-done.1 = bf16[27,64,64]{2,1,0:T(8,128)(2,1)S(1)} copy-done((bf16[27,64,64]{2,1,0:T(8,128)(2,1)S(1)}, bf16[27,64,64]{2,1,0:T(8,128)(2,1)}, u32[]{:S(2)}) %copy-start.1) | copy-done | bytes 221208
  2.7 0.0 copy-start.2
  2.7 1.0 %copy-done.2 = bf16[27,64,64]{2,1,0:T(8,128)(2,1)S(1)} copy-done((bf16[27,64,64]{2,1,0:T(8,128)(2,1)S(1)}, bf16[27,64,64]{2,1,0:T(8,128)(2,1)}, u32[]{:S(2)}) %copy-start.2) | copy-done | bytes 221208
  3.7 0.0 copy-start.3
  3.7 0.9 %copy-done.3 = bf16[8,64,64]{2,1,0:T(8,128)(2,1)S(1)} copy-done((bf16[8,64,64]{2,1,0:T(8,128)(2,1)S(1)}, bf16[8,64,64]{2,1,0:T(8,128)(2,1)}, u32[]{:S(2)}) %copy-start.3) | copy-done | bytes 65560
  4.6 0.0 copy-start.4
  4.6 0.9 %copy-done.4 = bf16[8,64,64]{2,1,0:T(8,128)(2,1)S(1)} copy-done((bf16[8,64,64]{2,1,0:T(8,128)(2,1)S(1)}, bf16[8,64,64]{2,1,0:T(8,128)(2,1)}, u32[]{:S(2)}) %copy-start.4) | copy-done | bytes 65560
  5.5 0.0 copy-start.5
  5.5 0.7 %copy-done.5 = s32[1,8]{1,0:T(1,128)S(1)} copy-done((s32[1,8]{1,0:T(1,128)S(1)}, s32[1,8]{1,0:T(1,128)}, u32[]{:S(2)}) %copy-start.5) | copy-done | bytes 56
  6.1 0.0 copy-start.6
  6.1 0.9 %copy-done.6 = bf16[512,128]{1,0:T(8,128)(2,1)S(1)} copy-done((bf16[512,128]{1,0:T(8,128)(2,1)S(1)}, bf16[512,128]{1,0:T(8,128)(2,1)}, u32[]{:S(2)}) %copy-start.6) | copy-done | bytes 131096
  7.0 0.0 copy-start.7
  7.0 0.9 %copy-done.7 = bf16[128,512]{1,0:T(8,128)(2,1)S(1)} copy-done((bf16[128,512]{1,0:T(8,128)(2,1)S(1)}, bf16[128,512]{1,0:T(8,128)(2,1)}, u32[]{:S(2)}) %copy-start.7) | copy-done | bytes 131096
  7.9 40.1 %shard_map.140 = (bf16[64,4,8,64]{3,2,1,0:T(8,128)(2,1)}, bf16[1,8,64,512]{3,2,1,0:T(8,128)(2,1)}) custom-call(bf16[64,4,8,64]{3,2,1,0:T(8,128)(2,1)} %fields.1, s32[1,8]{1,0:T(1,128)S(1)} %copy-done.5, bf16[1,8,64,512]{3,2,1,0:T(8,128)(2,1)} %fine.1, bf16[27,64,64]{2,1,0:T(8,128)(2,1)S(1)} %copy-done, bf16[8,64,64]{2,1,0:T(8,128)(2,1)S(1)} %copy-done.3, ...), custom_call_target="tpu_custom_call" | custom-call | flops 8000000000 | bytes 8000000 | tf_op jit(solution)/shard_map/pallas_call | solution.py:576
  48.0 1.9 %copy.17 = bf16[64,4,8,64]{3,2,1,0:T(8,128)(2,1)} copy(bf16[64,4,8,64]{3,2,1,0:T(8,128)(2,1)} %get-tuple-element.4) | data formatting | bytes 524288
  49.9 1.9 %copy.18 = bf16[1,8,64,512]{3,2,1,0:T(8,128)(2,1)} copy(bf16[1,8,64,512]{3,2,1,0:T(8,128)(2,1)} %get-tuple-element.5) | data formatting | bytes 1048576
Async XLA Ops:
  0.6 1.0 %copy-start = (bf16[27,64,64]{2,1,0:T(8,128)(2,1)S(1)}, bf16[27,64,64]{2,1,0:T(8,128)(2,1)}, u32[]{:S(2)}) copy-start(bf16[27,64,64]{2,1,0:T(8,128)(2,1)} %w_first.1) | copy-start | bytes 663556
  1.6 1.0 %copy-start.1 = (bf16[27,64,64]{2,1,0:T(8,128)(2,1)S(1)}, bf16[27,64,64]{2,1,0:T(8,128)(2,1)}, u32[]{:S(2)}) copy-start(bf16[27,64,64]{2,1,0:T(8,128)(2,1)} %w_coarse.1) | copy-start | bytes 663556
  2.7 1.0 %copy-start.2 = (bf16[27,64,64]{2,1,0:T(8,128)(2,1)S(1)}, bf16[27,64,64]{2,1,0:T(8,128)(2,1)}, u32[]{:S(2)}) copy-start(bf16[27,64,64]{2,1,0:T(8,128)(2,1)} %w_second.1) | copy-start | bytes 663556
  3.7 0.9 %copy-start.3 = (bf16[8,64,64]{2,1,0:T(8,128)(2,1)S(1)}, bf16[8,64,64]{2,1,0:T(8,128)(2,1)}, u32[]{:S(2)}) copy-start(bf16[8,64,64]{2,1,0:T(8,128)(2,1)} %w_restrict.1) | copy-start | bytes 196612
  4.6 0.9 %copy-start.4 = (bf16[8,64,64]{2,1,0:T(8,128)(2,1)S(1)}, bf16[8,64,64]{2,1,0:T(8,128)(2,1)}, u32[]{:S(2)}) copy-start(bf16[8,64,64]{2,1,0:T(8,128)(2,1)} %w_prolong.1) | copy-start | bytes 196612
  5.5 0.7 %copy-start.5 = (s32[1,8]{1,0:T(1,128)S(1)}, s32[1,8]{1,0:T(1,128)}, u32[]{:S(2)}) copy-start(s32[1,8]{1,0:T(1,128)} %patch.1) | copy-start | bytes 100
  6.1 0.9 %copy-start.6 = (bf16[512,128]{1,0:T(8,128)(2,1)S(1)}, bf16[512,128]{1,0:T(8,128)(2,1)}, u32[]{:S(2)}) copy-start(bf16[512,128]{1,0:T(8,128)(2,1)} %constant.10.clone.t_mean) | copy-start | bytes 393220
  7.0 0.9 %copy-start.7 = (bf16[128,512]{1,0:T(8,128)(2,1)S(1)}, bf16[128,512]{1,0:T(8,128)(2,1)}, u32[]{:S(2)}) copy-start(bf16[128,512]{1,0:T(8,128)(2,1)} %constant.9.clone.t_spread) | copy-start | bytes 393220
where the time goes:
time: 52.4 us; the launch traced here: 51.8 us
  Pallas kernels  40.1 us (77%)
  local copies, waits for them, and re-layouts  11 us (21%)
  between operations  0.66 us (1%)
    pallas_call x1, Pallas kernels, body(): pl.pallas_call(kernel, out_shape=[jax.ShapeDtypeStruct(fields.shape, BF),...  40.1 us
    unnamed x18, local copies, waits for them, and re-layouts  11 us

commit v1 on v0

v1 whole, which is shorter than its diff:
```python
import jax
import jax.numpy as jnp
import numpy as np
from jax import lax
from jax.experimental import pallas as pl
from jax.experimental.pallas import tpu as pltpu
from jax.sharding import PartitionSpec as P

BF = jnp.bfloat16
F32 = jnp.float32
MESH = pl.DeviceIdType.MESH
DIRS = [(dz, dy) for dz in (-1, 0, 1) for dy in (-1, 0, 1) if (dz, dy) != (0, 0)]


def split_table():
    cell = np.arange(512)
    row, col = cell // 64, cell % 64
    table = np.zeros((640, 512), np.float32)
    table[cell + 64, ((row % 2) * 2 + col % 2) * 128 + (row // 2) * 32 + col // 2] = 1
    return table


def spread_table():
    table = np.zeros((128, 512), np.float32)
    for q in range(2):
        for r in range(2):
            for k in range(32):
                table[k, (q * 2 + r) * 128 + (1 - q) * 64 + 2 * k + r] = 1
    return table


def mean_table():
    cell = np.arange(512)
    z, y, x = cell // 64, cell // 8 % 8, cell % 8
    table = np.zeros((512, 128), np.float32)
    table[cell, (z // 2) * 16 + (y // 2) * 4 + x // 2] = 0.125
    return table


def block_table():
    table = np.zeros((5, 256, 1152), np.float32)
    for m in range(5):
        for tap in range(9):
            for a in range(2):
                for b in range(8):
                    for e in range(8):
                        y, x = b + tap // 3 - 1, e + tap % 3 - 1
                        col = tap * 128 + a * 64 + b * 8 + e
                        ghost = (y // 2 + 1) * 6 + x // 2 + 1
                        if m == 4:
                            table[m, a * 128 + (0, 80)[a] + ghost, col] = 1
                        elif 0 <= y < 8 and 0 <= x < 8:
                            table[m, a * 64 + y * 8 + x, col] = 1
                        else:
                            table[m, 128 + 40 * ((m + 1) % 3) + ghost, col] = 1
    return table


def dot(a, b):
    return jnp.dot(a, b, preferred_element_type=F32)


def silu(v):
    return v / (1.0 + jnp.exp(-v))


def lanes_of(shape):
    return lax.broadcasted_iota(jnp.int32, shape, len(shape) - 1)


def splat(flag, shape):
    return jnp.full(shape, jnp.where(flag, 1.0, 0.0).astype(F32), F32)


def pack_taps(raw, packed):
    for dz in range(3):
        packed[dz * 64 : dz * 64 + 64, :] = jnp.concatenate(
            [raw[dz * 9 + t] for t in range(9)], axis=1
        )


def shifted(tile, period):
    lane = lanes_of(tile.shape) % period
    zero = jnp.zeros_like(tile)
    left = jnp.where(lane != 0, pltpu.roll(tile, 1, 1), zero)
    right = jnp.where(lane != period - 1, pltpu.roll(tile, 127, 1), zero)
    return left, tile, right


def stack_rows(tiles, x_ref, start):
    low = lanes_of((64, 128)) < 64
    moved = [shifted(t, 64) for t in tiles]
    for dx in range(3):
        swapped = [pltpu.roll(m[dx], 64, 1) for m in moved]
        for t in range(len(tiles) - 1):
            at = slice(start + t * 128, start + t * 128 + 128)
            x_ref[dx * 64 : dx * 64 + 64, at] = moved[t][dx]
            x_ref[192 + dx * 64 : 256 + dx * 64, at] = jnp.where(low, swapped[t], swapped[t + 1])
            x_ref[384 + dx * 64 : 448 + dx * 64, at] = moved[t + 1][dx]


def kernel(
    fields,
    patch,
    fine,
    w_first,
    w_restrict,
    w_coarse,
    w_prolong,
    w_second,
    w_refine,
    t_split,
    t_spread,
    t_mean,
    t_block,
    base_out,
    fine_out,
    fields_v,
    cells,
    field_t,
    raw_first,
    raw_restrict,
    raw_coarse,
    raw_prolong,
    raw_second,
    raw_refine,
    split_v,
    spread_v,
    mean_v,
    block_v,
    fine_i,
    fine_o,
    k_first,
    k_restrict,
    k_coarse,
    k_prolong,
    k_second,
    k_refine,
    lists,
    live_v,
    pick,
    place,
    x_v,
    y_v,
    act,
    summed,
    coarse_i,
    u_v,
    win,
    xf_v,
    load_sem,
    own_sem,
    store_sem,
    s_send,
    s_recv,
    c_send,
    c_recv,
    l_send,
    l_recv,
    f_send,
    f_recv,
    b_send,
    b_recv,
):
    g = lax.axis_index("gz")
    h = lax.axis_index("gx")
    n_g = lax.axis_size("gz")
    n_h = lax.axis_size("gx")

    def near(dz, dy):
        return (lax.rem(g + dz + n_g, n_g), lax.rem(h + dy + n_h, n_h))

    barrier = pltpu.get_barrier_semaphore()
    partners = DIRS + [(0, 2)]
    for dz, dy in partners:
        pl.semaphore_signal(barrier, inc=1, device_id=near(dz, dy), device_id_type=MESH)

    loads = []
    for i, (src, dst) in enumerate(
        [
            (fields, fields_v),
            (w_first, raw_first),
            (w_restrict, raw_restrict),
            (t_split, split_v),
            (w_refine, raw_refine),
            (t_block, block_v),
            (w_coarse, raw_coarse),
            (w_prolong, raw_prolong),
            (w_second, raw_second),
            (t_spread, spread_v),
            (t_mean, mean_v),
        ]
    ):
        loads.append(pltpu.make_async_copy(src, dst, load_sem.at[i]))
        loads[-1].start()
    own_fine = pltpu.make_async_copy(
        fine.at[0, pl.ds(2 * h, 2)], fine_i.at[h], own_sem.at[0]
    )
    own_fine.start()

    lists[h] = jnp.zeros((8, 128), jnp.int32)
    lists[h, 0:1, 0:8] = patch[...]

    loads[0].wait()
    cells[...] = fields_v[...].astype(F32).reshape(2048, 64)
    for z in range(4):
        for j in range(4):
            pair = [cells[pl.ds(z * 8 + 2 * j + q, 64, stride=32), :] for q in range(2)]
            field_t[2 + z, 1 + j] = jnp.concatenate(pair, axis=1).astype(BF)

    pl.semaphore_wait(barrier, len(partners))

    def span_of(d, own, width, low, high):
        if d == 0:
            return pl.ds(low, own), pl.ds(low, own)
        if d > 0:
            return pl.ds(low + own - width, width), pl.ds(low - width, width)
        return pl.ds(low, width), pl.ds(high, width)

    sends = {}
    for i, (dz, dy) in enumerate(DIRS):
        zs, zd = span_of(dz, 4, 2, 2, 6)
        ys, yd = span_of(dy, 4, 1, 1, 5)
        sends[dz, dy] = pltpu.make_async_remote_copy(
            src_ref=field_t.at[zs, ys],
            dst_ref=field_t.at[zd, yd],
            send_sem=s_send.at[i],
            recv_sem=s_recv.at[i],
            device_id=near(dz, dy),
            device_id_type=MESH,
        )
    order = [(-1, -1), (-1, 1), (1, -1), (1, 1), (0, -1), (0, 1), (-1, 0), (1, 0)]
    for d in order:
        sends[d].start()
    list_sends = []
    fine_sends = []
    for d in (2, 1, 3):
        peer = near(0, d)
        list_sends.append(
            pltpu.make_async_remote_copy(
                src_ref=lists.at[h],
                dst_ref=lists.at[h],
                send_sem=l_send.at[d - 1],
                recv_sem=l_recv.at[d - 1],
                device_id=peer,
                device_id_type=MESH,
            )
        )
        list_sends[-1].start()
    for d in (2, 1, 3):
        peer = near(0, d)
        fine_sends.append(
            pltpu.make_async_remote_copy(
                src_ref=fine.at[0, pl.ds(2 * peer[1], 2)],
                dst_ref=fine_i.at[h],
                send_sem=f_send.at[d - 1],
                recv_sem=f_recv.at[d - 1],
                device_id=peer,
                device_id_type=MESH,
            )
        )
        fine_sends[-1].start()

    first_z, last_z = g == 0, g == n_g - 1
    ok_low = splat(h != 0, (64, 128)).astype(BF)
    ok_high = splat(h != n_h - 1, (64, 128)).astype(BF)
    ok_first = splat(g != 0, (64, 128)).astype(BF)
    ok_last = splat(g != n_g - 1, (64, 128)).astype(BF)

    def field(p, t):
        tile = field_t[p, t]
        if t == 0:
            tile = tile * ok_low
        if t == 5:
            tile = tile * ok_high
        if p < 2:
            tile = tile * ok_first
        if p >= 6:
            tile = tile * ok_last
        return tile

    turn = [0]

    def conv_part(load, weight, runs):
        x_ref = x_v.at[turn[0] % 2]
        turn[0] += 1
        start = 0
        for p, first, last in runs:
            stack_rows([load(p, t) for t in range(first, last + 2)], x_ref, start)
            start += (last + 1 - first) * 128
        total = dot(weight[...], x_ref[:, 0:start])
        start = 0
        for p, first, last in runs:
            size = (last + 1 - first) * 128
            y_v[p, :, first * 128 : first * 128 + size] = total[:, start : start + size]
            start += size

    loads[1].wait()
    pack_taps(raw_first, k_first)
    conv_part(field, k_first, [(2, 1, 3), (3, 1, 3)])
    conv_part(field, k_first, [(4, 1, 3), (5, 1, 3)])

    for copy in loads[2:]:
        copy.wait()
    pack_taps(raw_coarse, k_coarse)
    pack_taps(raw_second, k_second)
    pack_taps(raw_refine, k_refine)
    k_restrict[...] = jnp.concatenate([raw_restrict[t] for t in range(8)], axis=1)
    for p in range(2):
        k_prolong[p * 64 : p * 64 + 64, :] = jnp.concatenate(
            [raw_prolong[p * 4 + t] for t in range(4)], axis=1
        )

    for copy in list_sends:
        copy.wait_recv()
    entry = lax.broadcasted_iota(jnp.int32, (8, 128), 1)
    lane = lanes_of((1, 128)).astype(F32)
    line = jnp.floor((lane + 0.5) * (1.0 / 6.0))
    place_x = lane - 6.0 * line - 1.0
    source = lax.broadcasted_iota(jnp.int32, (640, 128), 0).astype(F32)
    target = lanes_of((64, 512)).astype(F32)
    inner = (lax.broadcasted_iota(jnp.int32, (64, 1), 0) % 16).astype(F32)
    inner_y = jnp.floor(inner * 0.25)
    inner = inner_y * 64.0 + (inner - 4.0 * inner_y)
    for k in range(4):
        ids = lists[k].astype(F32)
        for s in range(2):
            at = k * 2 + s
            value = jnp.sum(
                jnp.where(entry == h * 2 + s, ids, 0.0), axis=1, keepdims=True
            )[0:1]
            py = jnp.floor(value * (1.0 / 16.0))
            px4 = 4.0 * (value - 16.0 * py)
            top = 256.0 * (py - 2.0 * h.astype(F32))
            col = place_x + px4
            want = jnp.where(
                (lane < 36.0) & (col >= 0.0) & (col < 64.0), line * 64.0 + col + top, -1.0
            )
            pick[:, at * 128 : at * 128 + 128] = jnp.where(source == want, 1.0, 0.0).astype(BF)
            want = jnp.where(value >= 0.0, inner + px4 + top, -1.0)
            place[at * 64 : at * 64 + 64, :] = jnp.where(target == want, 1.0, 0.0).astype(BF)
            live_v[k, s : s + 1, :] = jnp.where(
                jnp.broadcast_to(value, (1, 128)) >= 0.0, 1.0, 0.0
            )

    for d in ((0, -1), (0, 1)):
        sends[d].wait_recv()
    conv_part(field, k_first, [(p, t, t) for p in (2, 3, 4, 5) for t in (0, 4)])
    for d in order[:4] + order[6:]:
        sends[d].wait_recv()
    conv_part(field, k_first, [(0, 0, 4), (1, 0, 4)])
    conv_part(field, k_first, [(6, 0, 4), (7, 0, 4)])

    ok_rows = [jnp.ones((64, 128), F32)] * 5
    half = lanes_of((64, 128))
    ok_rows[0] = jnp.where((half < 64) & (h == 0), 0.0, 1.0)
    ok_rows[4] = jnp.where((half >= 64) & (h == n_h - 1), 0.0, 1.0)
    for q in range(6):
        for t in range(5):
            at = slice(t * 128, t * 128 + 128)
            value = silu(y_v[q, 0:64, at] + y_v[q + 1, 64:128, at] + y_v[q + 2, 128:192, at])
            if t in (0, 4):
                value = value * ok_rows[t]
            if q in (0, 5):
                value = value * splat(g != (0 if q == 0 else n_g - 1), (64, 128))
            act[q * 64 : q * 64 + 64, at] = value.astype(BF)

    parted = dot(act[64:320, :], split_v[...]).astype(BF)
    gathered = jnp.concatenate(
        [
            jnp.concatenate(
                [
                    parted[(2 * i + p) * 64 : (2 * i + p) * 64 + 64, f * 128 : f * 128 + 128]
                    for p in range(2)
                    for f in range(4)
                ],
                axis=0,
            )
            for i in range(2)
        ],
        axis=1,
    )
    reduced = dot(k_restrict[...], gathered).astype(BF)
    coarse_i[2, 1] = reduced[:, 0:128]
    coarse_i[3, 1] = reduced[:, 128:256]

    in_sends = []
    for i, (dz, dy) in enumerate(DIRS):
        in_sends.append(
            pltpu.make_async_remote_copy(
                src_ref=coarse_i.at[pl.ds(2, 2), pl.ds(1, 1)],
                dst_ref=coarse_i.at[pl.ds(2 - 2 * dz, 2), pl.ds(1 - dy, 1)],
                send_sem=c_send.at[i],
                recv_sem=c_recv.at[i],
                device_id=near(dz, dy),
                device_id_type=MESH,
            )
        )
    for i in (0, 2, 5, 7, 3, 4, 1, 6):
        in_sends[i].start()

    for k in range(4):
        found = dot(act[...], pick[:, k * 256 : k * 256 + 256])
        for s in range(2):
            parts = [found[q * 64 : q * 64 + 64, s * 128 : s * 128 + 128] for q in range(6)]
            for t in range(2):
                tile = (
                    parts[3 * t]
                    + pltpu.roll(parts[3 * t + 1], 40, 1)
                    + pltpu.roll(parts[3 * t + 2], 80, 1)
                )
                at = (k * 2 + s) * 64
                win[t, at : at + 64, :] = tile.astype(BF)

    own_fine.wait()
    for copy in fine_sends:
        copy.wait_recv()
    for m in range(5):
        if m < 4:
            left = fine_i[:, :, :, m * 128 : m * 128 + 128].reshape(512, 128)
            right = win[(m + 1) // 3]
        else:
            left = win[0]
            right = win[1]
        spread = dot(jnp.concatenate([left, right], axis=1), block_v[m]).astype(BF)
        for s in range(8):
            for tap in range(9):
                xf_v[s, tap * 64 : tap * 64 + 64, m * 128 : m * 128 + 128] = spread[
                    s * 64 : s * 64 + 64, tap * 128 : tap * 128 + 128
                ]

    low = lanes_of((64, 128)) < 64
    back_sends = []
    for s in range(8):
        total = dot(k_refine[...], xf_v[s])
        alive = jnp.broadcast_to(live_v[s // 2, s % 2 : s % 2 + 1, :], (64, 128)) > 0.5
        behind = [total[0:64, m * 128 : m * 128 + 128] for m in range(5)]
        ahead = [total[128:192, m * 128 : m * 128 + 128] for m in range(5)]
        behind_r = [pltpu.roll(v, 64, 1) for v in behind[:4]]
        ahead_r = [pltpu.roll(v, 64, 1) for v in ahead[:4]]
        for m in range(4):
            at = slice(m * 128, m * 128 + 128)
            value = total[64:128, at]
            value += jnp.where(low, behind_r[m - 1] if m > 0 else behind[4], behind_r[m])
            value += jnp.where(low, ahead_r[m], ahead_r[m + 1] if m < 3 else ahead[4])
            value += fine_i[s // 2, s % 2, :, at].astype(F32)
            value = jnp.where(alive, value, 0.0)
            fine_o[s // 2, s % 2, :, at] = value.astype(BF)

    for d in (2, 1, 3):
        peer = near(0, d)
        back_sends.append(
            pltpu.make_async_remote_copy(
                src_ref=fine_o.at[peer[1]],
                dst_ref=fine_out.at[0, pl.ds(2 * h, 2)],
                send_sem=b_send.at[d - 1],
                recv_sem=b_recv.at[d - 1],
                device_id=peer,
                device_id_type=MESH,
            )
        )
        back_sends[-1].start()
    own_store = pltpu.make_async_copy(
        fine_o.at[h], fine_out.at[0, pl.ds(2 * h, 2)], store_sem.at[0]
    )
    own_store.start()
    means = dot(fine_o[...].reshape(512, 512), mean_v[...])
    back = jnp.concatenate(
        [
            (
                means[k * 128 : k * 128 + 64]
                + pltpu.roll(means[k * 128 + 64 : k * 128 + 128], 64, 1)
            ).astype(BF)
            for k in range(4)
        ],
        axis=1,
    )
    wide = lanes_of((64, 512)) % 64 // 16
    zero = jnp.zeros_like(back)
    ones = jnp.where(lanes_of((16, 512)) % 64 < 16, 1.0, 0.0).astype(BF)
    stacked = jnp.concatenate([jnp.where(wide == z, back, zero) for z in range(4)] + [ones], axis=0)
    placed = dot(stacked, place[...])

    for copy in in_sends:
        copy.wait_recv()
    x_ref = x_v.at[turn[0] % 2]
    turn[0] += 1
    for i in range(6):
        before, mid, after = [coarse_i[i, t] for t in range(3)]
        if i < 2:
            before, mid, after = before * ok_first, mid * ok_first, after * ok_first
        if i >= 4:
            before, mid, after = before * ok_last, mid * ok_last, after * ok_last
        before, after = before * ok_low, after * ok_high
        around = [
            jnp.where(half < 64, pltpu.roll(before, 64, 1), pltpu.roll(mid, 64, 1)),
            jnp.where(half < 32, pltpu.roll(before, 32, 1), pltpu.roll(mid, 32, 1)),
            mid,
            jnp.where(half < 96, pltpu.roll(mid, 96, 1), pltpu.roll(after, 96, 1)),
            jnp.where(half < 64, pltpu.roll(mid, 64, 1), pltpu.roll(after, 64, 1)),
        ]
        for a, tile in enumerate(around):
            for dx, moved in enumerate(shifted(tile, 32)):
                for part, dy in ((0, a), (1, a - 2)):
                    if 0 <= dy < 3:
                        at = slice(i * 256 + part * 128, i * 256 + part * 128 + 128)
                        tap = dy * 3 + dx
                        x_ref[tap * 64 : tap * 64 + 64, at] = moved
    total = dot(k_coarse[...], x_ref[...])
    no_row = jnp.where((half < 32) & (h == 0), 0.0, 1.0)
    no_end = jnp.where((half >= 96) & (h == n_h - 1), 0.0, 1.0)
    rows = []
    for i in range(4):
        parts = []
        for part in range(2):
            at = i * 256 + part * 128
            value = silu(
                total[0:64, at : at + 128]
                + total[64:128, at + 256 : at + 384]
                + total[128:192, at + 512 : at + 640]
            )
            value = value * (no_row if part == 0 else no_end)
            if i in (0, 3):
                value = value * splat(g != (0 if i == 0 else n_g - 1), (64, 128))
            parts.append(value.astype(BF))
        rows += [parts[0]] + [pltpu.roll(parts[0], 128 - 32 * j, 1) for j in range(1, 4)]
        rows += [pltpu.roll(parts[1], 128 - 32 * j, 1) for j in range(2, 4)]
    spread = dot(jnp.concatenate(rows, axis=0), spread_v[...]).astype(BF)
    for i in range(4):
        for t in range(5):
            for f in range(4):
                row = (i * 6 + t + 1 - f // 2) * 64
                at = i * 640 + t * 128
                u_v[f * 64 : f * 64 + 64, at : at + 128] = spread[
                    row : row + 64, f * 128 : f * 128 + 128
                ]
    for i in range(4):
        lifted = dot(k_prolong[...], u_v[:, i * 640 : i * 640 + 640])
        for p in range(2):
            q = 2 * i - 1 + p
            if 0 <= q <= 5:
                at = slice(q * 64, q * 64 + 64)
                summed[at, :] = (
                    act[at, :].astype(F32) + lifted[p * 64 : p * 64 + 64, :]
                ).astype(BF)

    def total_in(q, t):
        return summed[q * 64 : q * 64 + 64, t * 128 : t * 128 + 128]

    for q in (0, 2, 4):
        conv_part(total_in, k_second, [(q, 0, 3), (q + 1, 0, 3)])

    for z in range(4):
        for j in range(4):
            at = slice(j * 128, j * 128 + 128)
            value = y_v[z, 0:64, at] + y_v[z + 1, 64:128, at] + y_v[z + 2, 128:192, at]
            value += field_t[2 + z, 1 + j].astype(F32)
            covered = jnp.broadcast_to(placed[256:257, at], (64, 128)) > 0.5
            value = jnp.where(covered, placed[z * 64 : z * 64 + 64, at], value)
            cells[pl.ds(z * 8 + 2 * j, 64, stride=32), :] = value[:, 0:64]
            cells[pl.ds(z * 8 + 2 * j + 1, 64, stride=32), :] = value[:, 64:128]
    fields_v[...] = cells[...].reshape(64, 4, 8, 64).astype(BF)
    base_store = pltpu.make_async_copy(fields_v, base_out, store_sem.at[1])
    base_store.start()
    for copy in back_sends:
        copy.wait_recv()
    for copy in list(sends.values()) + list_sends + fine_sends + in_sends + back_sends:
        copy.wait_send()
    own_store.wait()
    base_store.wait()


def body(
    fields,
    block_patch,
    fine_in,
    conv_first,
    restrict_weight,
    coarse_weight,
    prolong_weight,
    conv_second,
    refine_weight,
):
    any_spec = pl.BlockSpec(memory_space=pl.ANY)
    vmem_spec = pl.BlockSpec(memory_space=pltpu.VMEM)
    dma = pltpu.SemaphoreType.DMA
    v = pltpu.VMEM
    return pl.pallas_call(
        kernel,
        out_shape=[
            jax.ShapeDtypeStruct(fields.shape, BF),
            jax.ShapeDtypeStruct(fine_in.shape, BF),
        ],
        in_specs=[any_spec, vmem_spec] + [any_spec] * 11,
        out_specs=[any_spec, any_spec],
        scratch_shapes=[
            v((64, 4, 8, 64), BF),
            v((2048, 64), F32),
            v((8, 6, 64, 128), BF),
            v((27, 64, 64), BF),
            v((8, 64, 64), BF),
            v((27, 64, 64), BF),
            v((8, 64, 64), BF),
            v((27, 64, 64), BF),
            v((27, 64, 64), BF),
            v((640, 512), BF),
            v((128, 512), BF),
            v((512, 128), BF),
            v((5, 256, 1152), BF),
            v((4, 2, 64, 512), BF),
            v((4, 2, 64, 512), BF),
            v((192, 576), BF),
            v((64, 512), BF),
            v((192, 576), BF),
            v((128, 256), BF),
            v((192, 576), BF),
            v((192, 576), BF),
            v((4, 8, 128), jnp.int32),
            v((4, 8, 128), F32),
            v((640, 1024), BF),
            v((512, 512), BF),
            v((2, 576, 1536), BF),
            v((8, 192, 640), F32),
            v((384, 640), BF),
            v((384, 640), BF),
            v((6, 3, 64, 128), BF),
            v((256, 2560), BF),
            v((2, 512, 128), BF),
            v((8, 576, 640), BF),
            dma((11,)),
            dma((1,)),
            dma((2,)),
            dma((8,)),
            dma((8,)),
            dma((8,)),
            dma((8,)),
            dma((3,)),
            dma((3,)),
            dma((3,)),
            dma((3,)),
            dma((3,)),
            dma((3,)),
        ],
        compiler_params=pltpu.CompilerParams(
            collective_id=0, has_side_effects=True, vmem_limit_bytes=64 * 1024 * 1024
        ),
        cost_estimate=pl.CostEstimate(flops=8 * 10**9, bytes_accessed=8 * 10**6, transcendentals=0),
    )(
        fields,
        block_patch,
        fine_in,
        conv_first,
        restrict_weight,
        coarse_weight,
        prolong_weight,
        conv_second,
        refine_weight,
        jnp.asarray(split_table(), BF),
        jnp.asarray(spread_table(), BF),
        jnp.asarray(mean_table(), BF),
        jnp.asarray(block_table(), BF),
    )


def solution(mesh):
    in_specs = (
        P(None, "gz", "gx", None),
        P("gz", "gx"),
        P("gz", "gx", None, None),
        P(),
        P(),
        P(),
        P(),
        P(),
        P(),
    )
    out_specs = (P(None, "gz", "gx", None), P("gz", "gx", None, None))
    return jax.shard_map(body, mesh=mesh, in_specs=in_specs, out_specs=out_specs, check_vma=False)
```

time: 52.4 us -> 35.2 us (0.67)
  Pallas kernels: 40.1 us -> 30.3 us
  local copies, waits for them, and re-layouts: 11 us -> 3.74 us
    pallas_call x1, Pallas kernels: 40.1 us -> 30.3 us  [body(): pl.pallas_call(kernel, out_shape=[jax.ShapeDtypeStruct(fields.shape, BF),...]
    unnamed x18 -> x2, local copies, waits for them, and re-layouts: 11 us -> 3.74 us
where the time goes in v1:
time: 35.2 us; the launch traced here: 34.7 us
  Pallas kernels  30.3 us (86%)
  local copies, waits for them, and re-layouts  3.74 us (11%)
  between operations  0.64 us (2%)
    pallas_call x1, Pallas kernels, body(): pl.pallas_call(kernel, out_shape=[jax.ShapeDtypeStruct(fields.shape, BF),...  30.3 us
    unnamed x2, local copies, waits for them, and re-layouts  3.74 us

profile of v1, /device:TPU:0, one launch (start us, length us, event | category | flops | bytes accessed | tf_op | source)
XLA Modules:
  0.0 34.7 jit_solution(12507611390495995223)
XLA Ops:
  0.6 30.3 %shard_map.140 = (bf16[64,4,8,64]{3,2,1,0:T(8,128)(2,1)}, bf16[1,8,64,512]{3,2,1,0:T(8,128)(2,1)}) custom-call(bf16[64,4,8,64]{3,2,1,0:T(8,128)(2,1)} %fields.1, s32[1,8]{1,0:T(1,128)} %patch.1, bf16[1,8,64,512]{3,2,1,0:T(8,128)(2,1)} %fine.1, bf16[27,64,64]{2,1,0:T(8,128)(2,1)} %w_first.1, bf16[8,64,64]{2,1,0:T(8,128)(2,1)} %w_restrict.1, ...), custom_call_target="tpu_custom_call" | custom-call | flops 8000000000 | bytes 8000000 | tf_op jit(solution)/shard_map/pallas_call | solution.py:588
  30.9 1.9 %copy.17 = bf16[64,4,8,64]{3,2,1,0:T(8,128)(2,1)} copy(bf16[64,4,8,64]{3,2,1,0:T(8,128)(2,1)} %get-tuple-element.4) | data formatting | bytes 524288
  32.8 1.9 %copy.18 = bf16[1,8,64,512]{3,2,1,0:T(8,128)(2,1)} copy(bf16[1,8,64,512]{3,2,1,0:T(8,128)(2,1)} %get-tuple-element.5) | data formatting | bytes 1048576

commit v2 on v1

--- a/solution.py
+++ b/solution.py
@@ -192,16 +192,17 @@
         ]
     ):
         loads.append(pltpu.make_async_copy(src, dst, load_sem.at[i]))
-        loads[-1].start()
+    loads[0].start()
     own_fine = pltpu.make_async_copy(
         fine.at[0, pl.ds(2 * h, 2)], fine_i.at[h], own_sem.at[0]
     )
-    own_fine.start()
 
     lists[h] = jnp.zeros((8, 128), jnp.int32)
     lists[h, 0:1, 0:8] = patch[...]
 
     loads[0].wait()
+    for copy in loads[1:] + [own_fine]:
+        copy.start()
     cells[...] = fields_v[...].astype(F32).reshape(2048, 64)
     for z in range(4):
         for j in range(4):
@@ -247,6 +248,47 @@
             )
         )
         list_sends[-1].start()
+    first_z, last_z = g == 0, g == n_g - 1
+    ok_low = splat(h != 0, (64, 128)).astype(BF)
+    ok_high = splat(h != n_h - 1, (64, 128)).astype(BF)
+    ok_first = splat(g != 0, (64, 128)).astype(BF)
+    ok_last = splat(g != n_g - 1, (64, 128)).astype(BF)
+
+    def field(p, t):
+        tile = field_t[p, t]
+        if t == 0:
+            tile = tile * ok_low
+        if t == 5:
+            tile = tile * ok_high
+        if p < 2:
+            tile = tile * ok_first
+        if p >= 6:
+            tile = tile * ok_last
+        return tile
+
+    turn = [0]
+
+    def conv_part(load, weight, runs):
+        x_ref = x_v.at[turn[0] % 2]
+        turn[0] += 1
+        start = 0
+        for p, first, last in runs:
+            stack_rows([load(p, t) for t in range(first, last + 2)], x_ref, start)
+            start += (last + 1 - first) * 128
+        total = dot(weight[...], x_ref[:, 0:start])
+        start = 0
+        for p, first, last in runs:
+            size = (last + 1 - first) * 128
+            y_v[p, :, first * 128 : first * 128 + size] = total[:, start : start + size]
+            start += size
+
+    loads[1].wait()
+    pack_taps(raw_first, k_first)
+    conv_part(field, k_first, [(2, 1, 3), (3, 1, 3)])
+    conv_part(field, k_first, [(4, 1, 3), (5, 1, 3)])
+
+    for d in order:
+        sends[d].wait_send()
     for d in (2, 1, 3):
         peer = near(0, d)
         fine_sends.append(
@@ -261,44 +303,6 @@
         )
         fine_sends[-1].start()
 
-    first_z, last_z = g == 0, g == n_g - 1
-    ok_low = splat(h != 0, (64, 128)).astype(BF)
-    ok_high = splat(h != n_h - 1, (64, 128)).astype(BF)
-    ok_first = splat(g != 0, (64, 128)).astype(BF)
-    ok_last = splat(g != n_g - 1, (64, 128)).astype(BF)
-
-    def field(p, t):
-        tile = field_t[p, t]
-        if t == 0:
-            tile = tile * ok_low
-        if t == 5:
-            tile = tile * ok_high
-        if p < 2:
-            tile = tile * ok_first
-        if p >= 6:
-            tile = tile * ok_last
-        return tile
-
-    turn = [0]
-
-    def conv_part(load, weight, runs):
-        x_ref = x_v.at[turn[0] % 2]
-        turn[0] += 1
-        start = 0
-        for p, first, last in runs:
-            stack_rows([load(p, t) for t in range(first, last + 2)], x_ref, start)
-            start += (last + 1 - first) * 128
-        total = dot(weight[...], x_ref[:, 0:start])
-        start = 0
-        for p, first, last in runs:
-            size = (last + 1 - first) * 128
-            y_v[p, :, first * 128 : first * 128 + size] = total[:, start : start + size]
-            start += size
-
-    loads[1].wait()
-    pack_taps(raw_first, k_first)
-    conv_part(field, k_first, [(2, 1, 3), (3, 1, 3)])
-    conv_part(field, k_first, [(4, 1, 3), (5, 1, 3)])
 
     for copy in loads[2:]:
         copy.wait()
@@ -431,27 +435,29 @@
 
     low = lanes_of((64, 128)) < 64
     back_sends = []
-    for s in range(8):
-        total = dot(k_refine[...], xf_v[s])
-        alive = jnp.broadcast_to(live_v[s // 2, s % 2 : s % 2 + 1, :], (64, 128)) > 0.5
-        behind = [total[0:64, m * 128 : m * 128 + 128] for m in range(5)]
-        ahead = [total[128:192, m * 128 : m * 128 + 128] for m in range(5)]
-        behind_r = [pltpu.roll(v, 64, 1) for v in behind[:4]]
-        ahead_r = [pltpu.roll(v, 64, 1) for v in ahead[:4]]
-        for m in range(4):
-            at = slice(m * 128, m * 128 + 128)
-            value = total[64:128, at]
-            value += jnp.where(low, behind_r[m - 1] if m > 0 else behind[4], behind_r[m])
-            value += jnp.where(low, ahead_r[m], ahead_r[m + 1] if m < 3 else ahead[4])
-            value += fine_i[s // 2, s % 2, :, at].astype(F32)
-            value = jnp.where(alive, value, 0.0)
-            fine_o[s // 2, s % 2, :, at] = value.astype(BF)
-
-    for d in (2, 1, 3):
+    for d in (2, 1, 3, 0):
         peer = near(0, d)
+        k = peer[1]
+        for s in range(2):
+            total = dot(k_refine[...], xf_v[k * 2 + s])
+            alive = jnp.broadcast_to(live_v[k, s : s + 1, :], (64, 128)) > 0.5
+            behind = [total[0:64, m * 128 : m * 128 + 128] for m in range(5)]
+            ahead = [total[128:192, m * 128 : m * 128 + 128] for m in range(5)]
+            behind_r = [pltpu.roll(v, 64, 1) for v in behind[:4]]
+            ahead_r = [pltpu.roll(v, 64, 1) for v in ahead[:4]]
+            for m in range(4):
+                at = slice(m * 128, m * 128 + 128)
+                value = total[64:128, at]
+                value += jnp.where(low, behind_r[m - 1] if m > 0 else behind[4], behind_r[m])
+                value += jnp.where(low, ahead_r[m], ahead_r[m + 1] if m < 3 else ahead[4])
+                value += fine_i[k, s, :, at].astype(F32)
+                value = jnp.where(alive, value, 0.0)
+                fine_o[k, s, :, at] = value.astype(BF)
+        if d == 0:
+            continue
         back_sends.append(
             pltpu.make_async_remote_copy(
-                src_ref=fine_o.at[peer[1]],
+                src_ref=fine_o.at[k],
                 dst_ref=fine_out.at[0, pl.ds(2 * h, 2)],
                 send_sem=b_send.at[d - 1],
                 recv_sem=b_recv.at[d - 1],
@@ -564,10 +570,30 @@
     base_store.start()
     for copy in back_sends:
         copy.wait_recv()
-    for copy in list(sends.values()) + list_sends + fine_sends + in_sends + back_sends:
+    for copy in list_sends + fine_sends + in_sends + back_sends:
         copy.wait_send()
     own_store.wait()
     base_store.wait()
+
+
+def finish(base, fine, base_out, fine_out, base_v, fine_v, in_sems, out_sems):
+    loads = []
+    stores = []
+    for i in range(4):
+        parts = [
+            (base, base_v, base_out, (pl.ds(16 * i, 16),)),
+            (fine, fine_v, fine_out, (pl.ds(0, 1), pl.ds(2 * i, 2))),
+        ]
+        for j, (src, mid, dst, at) in enumerate(parts):
+            loads.append(pltpu.make_async_copy(src.at[at], mid.at[at], in_sems.at[2 * i + j]))
+            stores.append(pltpu.make_async_copy(mid.at[at], dst.at[at], out_sems.at[2 * i + j]))
+    for copy in loads:
+        copy.start()
+    for load, store in zip(loads, stores):
+        load.wait()
+        store.start()
+    for copy in stores:
+        copy.wait()
 
 
 def body(
@@ -585,7 +611,7 @@
     vmem_spec = pl.BlockSpec(memory_space=pltpu.VMEM)
     dma = pltpu.SemaphoreType.DMA
     v = pltpu.VMEM
-    return pl.pallas_call(
+    results = pl.pallas_call(
         kernel,
         out_shape=[
             jax.ShapeDtypeStruct(fields.shape, BF),
@@ -660,6 +686,22 @@
         jnp.asarray(mean_table(), BF),
         jnp.asarray(block_table(), BF),
     )
+    return pl.pallas_call(
+        finish,
+        out_shape=[
+            jax.ShapeDtypeStruct(fields.shape, BF),
+            jax.ShapeDtypeStruct(fine_in.shape, BF),
+        ],
+        in_specs=[any_spec, any_spec],
+        out_specs=[any_spec, any_spec],
+        scratch_shapes=[
+            v(fields.shape, BF),
+            v(fine_in.shape, BF),
+            dma((8,)),
+            dma((8,)),
+        ],
+        compiler_params=pltpu.CompilerParams(vmem_limit_bytes=64 * 1024 * 1024),
+    )(*results)
 
 
 def solution(mesh):

time: 35.2 us -> 32.3 us (0.918); the launches traced: 34.7 us -> 32.1 us
  local copies, waits for them, and re-layouts: 3.74 us -> 0 us
  Pallas kernels: 30.3 us -> 31.5 us
    unnamed x2 -> x0, local copies, waits for them, and re-layouts: 3.74 us -> none
    pallas_call x0 -> x1, Pallas kernels: none -> 2.09 us  [body(): pl.pallas_call(finish, out_shape=[jax.ShapeDtypeStruct(fields.shape, BF),...]
    pallas_call x1, Pallas kernels: 30.3 us -> 29.4 us  [body(): pl.pallas_call(kernel, out_shape=[jax.ShapeDtypeStruct(fields.shape, BF),...]
where the time goes in v2:
time: 32.3 us; the launch traced here: 32.1 us
  Pallas kernels  31.5 us (98%)
  between operations  0.64 us (2%)
    pallas_call x1, Pallas kernels, body(): pl.pallas_call(kernel, out_shape=[jax.ShapeDtypeStruct(fields.shape, BF),...  29.4 us
    pallas_call x1, Pallas kernels, body(): pl.pallas_call(finish, out_shape=[jax.ShapeDtypeStruct(fields.shape, BF),...  2.09 us

profile of v2, /device:TPU:0, one launch (start us, length us, event | category | flops | bytes accessed | tf_op | source)
XLA Modules:
  0.0 32.1 jit_solution(17351288331049178773)
XLA Ops:
  0.6 29.4 %shard_map.140 = (bf16[64,4,8,64]{3,2,1,0:T(8,128)(2,1)}, bf16[1,8,64,512]{3,2,1,0:T(8,128)(2,1)}) custom-call(bf16[64,4,8,64]{3,2,1,0:T(8,128)(2,1)} %fields.1, s32[1,8]{1,0:T(1,128)} %patch.1, bf16[1,8,64,512]{3,2,1,0:T(8,128)(2,1)} %fine.1, bf16[27,64,64]{2,1,0:T(8,128)(2,1)} %w_first.1, bf16[8,64,64]{2,1,0:T(8,128)(2,1)} %w_restrict.1, ...), custom_call_target="tpu_custom_call" | custom-call | flops 8000000000 | bytes 8000000 | tf_op jit(solution)/shard_map/pallas_call | solution.py:614
  30.0 2.1 %shard_map.141 = (bf16[64,4,8,64]{3,2,1,0:T(8,128)(2,1)}, bf16[1,8,64,512]{3,2,1,0:T(8,128)(2,1)}) custom-call(bf16[64,4,8,64]{3,2,1,0:T(8,128)(2,1)} %get-tuple-element.4.base, bf16[1,8,64,512]{3,2,1,0:T(8,128)(2,1)} %get-tuple-element.5.fine), custom_call_target="tpu_custom_call" | custom-call | tf_op jit(solution)/shard_map/pallas_call | solution.py:689

commit v3 on v2

--- a/solution.py
+++ b/solution.py
@@ -145,6 +145,8 @@
     act,
     summed,
     coarse_i,
+    edge_o,
+    edge_i,
     u_v,
     win,
     xf_v,
@@ -285,9 +287,7 @@
     loads[1].wait()
     pack_taps(raw_first, k_first)
     conv_part(field, k_first, [(2, 1, 3), (3, 1, 3)])
-    conv_part(field, k_first, [(4, 1, 3), (5, 1, 3)])
-
-    for d in order:
+    for d in order[:6]:
         sends[d].wait_send()
     for d in (2, 1, 3):
         peer = near(0, d)
@@ -303,6 +303,7 @@
         )
         fine_sends[-1].start()
 
+    conv_part(field, k_first, [(4, 1, 3), (5, 1, 3)])
 
     for copy in loads[2:]:
         copy.wait()
@@ -385,15 +386,22 @@
         axis=1,
     )
     reduced = dot(k_restrict[...], gathered).astype(BF)
-    coarse_i[2, 1] = reduced[:, 0:128]
-    coarse_i[3, 1] = reduced[:, 128:256]
-
+    low = half < 64
+    one, two = reduced[:, 0:128], reduced[:, 128:256]
+    coarse_i[2] = one
+    coarse_i[3] = two
+    edge_o[0] = jnp.where(low, one, pltpu.roll(two, 64, 1))
+    edge_o[1] = jnp.where(low, pltpu.roll(one, 64, 1), two)
     in_sends = []
     for i, (dz, dy) in enumerate(DIRS):
+        if dy == 0:
+            src, dst = coarse_i.at[pl.ds(2, 2)], coarse_i.at[pl.ds(2 - 2 * dz, 2)]
+        else:
+            src, dst = edge_o.at[(1 + dy) // 2], edge_i.at[(1 - dy) // 2, 1 - dz]
         in_sends.append(
             pltpu.make_async_remote_copy(
-                src_ref=coarse_i.at[pl.ds(2, 2), pl.ds(1, 1)],
-                dst_ref=coarse_i.at[pl.ds(2 - 2 * dz, 2), pl.ds(1 - dy, 1)],
+                src_ref=src,
+                dst_ref=dst,
                 send_sem=c_send.at[i],
                 recv_sem=c_recv.at[i],
                 device_id=near(dz, dy),
@@ -492,18 +500,21 @@
     x_ref = x_v.at[turn[0] % 2]
     turn[0] += 1
     for i in range(6):
-        before, mid, after = [coarse_i[i, t] for t in range(3)]
+        before, mid, after = edge_i[0, i // 2], coarse_i[i], edge_i[1, i // 2]
         if i < 2:
             before, mid, after = before * ok_first, mid * ok_first, after * ok_first
         if i >= 4:
             before, mid, after = before * ok_last, mid * ok_last, after * ok_last
         before, after = before * ok_low, after * ok_high
+        mid_r = pltpu.roll(mid, 64, 1)
         around = [
-            jnp.where(half < 64, pltpu.roll(before, 64, 1), pltpu.roll(mid, 64, 1)),
-            jnp.where(half < 32, pltpu.roll(before, 32, 1), pltpu.roll(mid, 32, 1)),
+            jnp.where(low, pltpu.roll(before, 64, 1) if i % 2 else before, mid_r),
+            jnp.where(
+                half < 32, pltpu.roll(before, 32 if i % 2 else 96, 1), pltpu.roll(mid, 32, 1)
+            ),
             mid,
-            jnp.where(half < 96, pltpu.roll(mid, 96, 1), pltpu.roll(after, 96, 1)),
-            jnp.where(half < 64, pltpu.roll(mid, 64, 1), pltpu.roll(after, 64, 1)),
+            jnp.where(half < 96, pltpu.roll(mid, 96, 1), pltpu.roll(after, 32 if i % 2 else 96, 1)),
+            jnp.where(low, mid_r, after if i % 2 else pltpu.roll(after, 64, 1)),
         ]
         for a, tile in enumerate(around):
             for dx, moved in enumerate(shifted(tile, 32)):
@@ -570,6 +581,8 @@
     base_store.start()
     for copy in back_sends:
         copy.wait_recv()
+    for d in order[6:]:
+        sends[d].wait_send()
     for copy in list_sends + fine_sends + in_sends + back_sends:
         copy.wait_send()
     own_store.wait()
@@ -649,7 +662,9 @@
             v((8, 192, 640), F32),
             v((384, 640), BF),
             v((384, 640), BF),
-            v((6, 3, 64, 128), BF),
+            v((6, 64, 128), BF),
+            v((2, 64, 128), BF),
+            v((2, 3, 64, 128), BF),
             v((256, 2560), BF),
             v((2, 512, 128), BF),
             v((8, 576, 640), BF),

time: 32.3 us -> 31.6 us (0.978)
  Pallas kernels: 31.5 us -> 30.8 us
    pallas_call x1, Pallas kernels: 29.4 us -> 28.7 us  [body(): pl.pallas_call(kernel, out_shape=[jax.ShapeDtypeStruct(fields.shape, BF),...]
where the time goes in v3:
time: 31.6 us; the launch traced here: 31.4 us
  Pallas kernels  30.8 us (97%)
  between operations  0.64 us (2%)
    pallas_call x1, Pallas kernels, body(): pl.pallas_call(kernel, out_shape=[jax.ShapeDtypeStruct(fields.shape, BF),...  28.7 us
    pallas_call x1, Pallas kernels, body(): pl.pallas_call(finish, out_shape=[jax.ShapeDtypeStruct(fields.shape, BF),...  2.09 us

profile of v3, /device:TPU:0, one launch (start us, length us, event | category | flops | bytes accessed | tf_op | source)
XLA Modules:
  0.0 31.4 jit_solution(10762778126145414795)
XLA Ops:
  0.6 28.7 %shard_map.140 = (bf16[64,4,8,64]{3,2,1,0:T(8,128)(2,1)}, bf16[1,8,64,512]{3,2,1,0:T(8,128)(2,1)}) custom-call(bf16[64,4,8,64]{3,2,1,0:T(8,128)(2,1)} %fields.1, s32[1,8]{1,0:T(1,128)} %patch.1, bf16[1,8,64,512]{3,2,1,0:T(8,128)(2,1)} %fine.1, bf16[27,64,64]{2,1,0:T(8,128)(2,1)} %w_first.1, bf16[8,64,64]{2,1,0:T(8,128)(2,1)} %w_restrict.1, ...), custom_call_target="tpu_custom_call" | custom-call | flops 8000000000 | bytes 8000000 | tf_op jit(solution)/shard_map/pallas_call | solution.py:627
  29.3 2.1 %shard_map.141 = (bf16[64,4,8,64]{3,2,1,0:T(8,128)(2,1)}, bf16[1,8,64,512]{3,2,1,0:T(8,128)(2,1)}) custom-call(bf16[64,4,8,64]{3,2,1,0:T(8,128)(2,1)} %get-tuple-element.4.base, bf16[1,8,64,512]{3,2,1,0:T(8,128)(2,1)} %get-tuple-element.5.fine), custom_call_target="tpu_custom_call" | custom-call | tf_op jit(solution)/shard_map/pallas_call | solution.py:704

commit v4 on v3

--- a/solution.py
+++ b/solution.py
@@ -427,27 +427,42 @@
     own_fine.wait()
     for copy in fine_sends:
         copy.wait_recv()
-    for m in range(5):
-        if m < 4:
-            left = fine_i[:, :, :, m * 128 : m * 128 + 128].reshape(512, 128)
-            right = win[(m + 1) // 3]
-        else:
-            left = win[0]
-            right = win[1]
-        spread = dot(jnp.concatenate([left, right], axis=1), block_v[m]).astype(BF)
-        for s in range(8):
-            for tap in range(9):
-                xf_v[s, tap * 64 : tap * 64 + 64, m * 128 : m * 128 + 128] = spread[
-                    s * 64 : s * 64 + 64, tap * 128 : tap * 128 + 128
-                ]
+    def spread_blocks(d_first, d_second):
+        ks = [near(0, d)[1] for d in (d_first, d_second)]
+        sides = [
+            jnp.concatenate([win[t, pl.ds(pl.multiple_of(k * 128, 128), 128), :] for k in ks], axis=0)
+            for t in range(2)
+        ]
+        for m in range(5):
+            if m < 4:
+                left = jnp.concatenate(
+                    [
+                        fine_i[k, :, :, m * 128 : m * 128 + 128].reshape(128, 128)
+                        for k in ks
+                    ],
+                    axis=0,
+                )
+                right = sides[(m + 1) // 3]
+            else:
+                left, right = sides
+            spread = dot(jnp.concatenate([left, right], axis=1), block_v[m]).astype(BF)
+            for i, d in enumerate((d_first, d_second)):
+                for s in range(2):
+                    row = i * 128 + s * 64
+                    for tap in range(9):
+                        xf_v[d * 2 + s, tap * 64 : tap * 64 + 64, m * 128 : m * 128 + 128] = spread[
+                            row : row + 64, tap * 128 : tap * 128 + 128
+                        ]
 
     low = lanes_of((64, 128)) < 64
     back_sends = []
     for d in (2, 1, 3, 0):
+        if d in (2, 3):
+            spread_blocks(d, 1 if d == 2 else 0)
         peer = near(0, d)
         k = peer[1]
         for s in range(2):
-            total = dot(k_refine[...], xf_v[k * 2 + s])
+            total = dot(k_refine[...], xf_v[d * 2 + s])
             alive = jnp.broadcast_to(live_v[k, s : s + 1, :], (64, 128)) > 0.5
             behind = [total[0:64, m * 128 : m * 128 + 128] for m in range(5)]
             ahead = [total[128:192, m * 128 : m * 128 + 128] for m in range(5)]

time: 31.6 us -> 31.5 us (level)
  no operation moved by 1% of the time
where the time goes in v4:
time: 31.5 us; the launch traced here: 31.3 us
  Pallas kernels  30.7 us (97%)
  between operations  0.64 us (2%)
    pallas_call x1, Pallas kernels, body(): pl.pallas_call(kernel, out_shape=[jax.ShapeDtypeStruct(fields.shape, BF),...  28.6 us
    pallas_call x1, Pallas kernels, body(): pl.pallas_call(finish, out_shape=[jax.ShapeDtypeStruct(fields.shape, BF),...  2.09 us

profile of v4, /device:TPU:0, one launch (start us, length us, event | category | flops | bytes accessed | tf_op | source)
XLA Modules:
  0.0 31.3 jit_solution(13143720022927590384)
XLA Ops:
  0.6 28.6 %shard_map.140 = (bf16[64,4,8,64]{3,2,1,0:T(8,128)(2,1)}, bf16[1,8,64,512]{3,2,1,0:T(8,128)(2,1)}) custom-call(bf16[64,4,8,64]{3,2,1,0:T(8,128)(2,1)} %fields.1, s32[1,8]{1,0:T(1,128)} %patch.1, bf16[1,8,64,512]{3,2,1,0:T(8,128)(2,1)} %fine.1, bf16[27,64,64]{2,1,0:T(8,128)(2,1)} %w_first.1, bf16[8,64,64]{2,1,0:T(8,128)(2,1)} %w_restrict.1, ...), custom_call_target="tpu_custom_call" | custom-call | flops 8000000000 | bytes 8000000 | tf_op jit(solution)/shard_map/pallas_call | solution.py:642
  29.2 2.1 %shard_map.141 = (bf16[64,4,8,64]{3,2,1,0:T(8,128)(2,1)}, bf16[1,8,64,512]{3,2,1,0:T(8,128)(2,1)}) custom-call(bf16[64,4,8,64]{3,2,1,0:T(8,128)(2,1)} %get-tuple-element.4.base, bf16[1,8,64,512]{3,2,1,0:T(8,128)(2,1)} %get-tuple-element.5.fine), custom_call_target="tpu_custom_call" | custom-call | tf_op jit(solution)/shard_map/pallas_call | solution.py:719

commit v5 on v4

--- a/solution.py
+++ b/solution.py
@@ -286,7 +286,6 @@
 
     loads[1].wait()
     pack_taps(raw_first, k_first)
-    conv_part(field, k_first, [(2, 1, 3), (3, 1, 3)])
     for d in order[:6]:
         sends[d].wait_send()
     for d in (2, 1, 3):
@@ -303,6 +302,7 @@
         )
         fine_sends[-1].start()
 
+    conv_part(field, k_first, [(2, 1, 3), (3, 1, 3)])
     conv_part(field, k_first, [(4, 1, 3), (5, 1, 3)])
 
     for copy in loads[2:]:

time: 31.5 us -> 31.5 us (level)
  no operation moved by 1% of the time
where the time goes in v5:
time: 31.5 us; the launch traced here: 31.3 us
  Pallas kernels  30.7 us (97%)
  between operations  0.64 us (2%)
    pallas_call x1, Pallas kernels, body(): pl.pallas_call(kernel, out_shape=[jax.ShapeDtypeStruct(fields.shape, BF),...  28.6 us
    pallas_call x1, Pallas kernels, body(): pl.pallas_call(finish, out_shape=[jax.ShapeDtypeStruct(fields.shape, BF),...  2.09 us

profile of v5, /device:TPU:0, one launch (start us, length us, event | category | flops | bytes accessed | tf_op | source)
XLA Modules:
  0.0 31.3 jit_solution(11013536913912597531)
XLA Ops:
  0.6 28.6 %shard_map.140 = (bf16[64,4,8,64]{3,2,1,0:T(8,128)(2,1)}, bf16[1,8,64,512]{3,2,1,0:T(8,128)(2,1)}) custom-call(bf16[64,4,8,64]{3,2,1,0:T(8,128)(2,1)} %fields.1, s32[1,8]{1,0:T(1,128)} %patch.1, bf16[1,8,64,512]{3,2,1,0:T(8,128)(2,1)} %fine.1, bf16[27,64,64]{2,1,0:T(8,128)(2,1)} %w_first.1, bf16[8,64,64]{2,1,0:T(8,128)(2,1)} %w_restrict.1, ...), custom_call_target="tpu_custom_call" | custom-call | flops 8000000000 | bytes 8000000 | tf_op jit(solution)/shard_map/pallas_call | solution.py:642
  29.2 2.1 %shard_map.141 = (bf16[64,4,8,64]{3,2,1,0:T(8,128)(2,1)}, bf16[1,8,64,512]{3,2,1,0:T(8,128)(2,1)}) custom-call(bf16[64,4,8,64]{3,2,1,0:T(8,128)(2,1)} %get-tuple-element.4.base, bf16[1,8,64,512]{3,2,1,0:T(8,128)(2,1)} %get-tuple-element.5.fine), custom_call_target="tpu_custom_call" | custom-call | tf_op jit(solution)/shard_map/pallas_call | solution.py:719
